TPU v7x, 256 devices: a whole 4x4x8 slice. The times are simulated.
256 devices in a mesh: ctx: 64 (over z, x, core), dp: 4 (over y).
Axes of the slice: x: 4, y: 4, z: 8, core: 2. Of those that a mesh axis runs over, the one named last changes fastest.
Arguments:
- query_in: bfloat16 [4, 16384, 4096], P('dp', 'ctx'), may hold values from -6 to 6
- key_in: bfloat16 [4, 16384, 512], P('dp', 'ctx'), may hold values from -6 to 6
- value_rows_input: bfloat16 [4, 16384, 512], P('dp', 'ctx'), may hold values from -6 to 6
- grad_out: bfloat16 [4, 16384, 4096], P('dp', 'ctx'), may hold values from -12 to 12
- query_bias: float32 [4096], replicated, may hold values from -1.5 to 1.5
- key_blocks: int32 [4, 128, 6], P('dp'), may hold values from -1 to 127, as said below
- trace_len: int32 [4], P('dp'), may hold values from 8192 to 16384, as said below
Outputs:
- grad_query: bfloat16 [4, 16384, 4096], P('dp', 'ctx')
- grad_key: bfloat16 [4, 16384, 512], P('dp', 'ctx')
- grad_value: bfloat16 [4, 16384, 512], P('dp', 'ctx')
- bias_grad: float32 [4096], replicated
Inputs may be any that keep to these rules, and one draw needn't show every extreme that they name: `key_blocks`: blocks are numbered by position. Entry 2 + d of query block q's list is q - d or -1, and entry 2 is always q; entry r < 2 is r or -1, and -1 whenever r >= q - 3. `trace_len`: some trace has 16384 tokens and some 16384 // 2.
All inputs are finite; a program needn't handle non-finite values.
Results may differ from a plain program's by a relative error of at most 0.011.
The roundings to bfloat16 on the way count: a program that leaves them out, or rounds other values in their place, can miss the bound.
Values may be sent and summed in bfloat16 or wider, within the bound.
A program may use at most 128 MiB of HBM per device.

v0:
```python
import math
import jax
import jax.numpy as jnp
from jax import lax
from jax.sharding import PartitionSpec as P

HEAD_SIZE = 128
BLOCK = 128
PROMPT = 2
WINDOW = 3


def from_behind(value, axis, steps):
    count = lax.axis_size(axis)
    initial, last = (max(0, -steps), min(count, count - steps))
    return lax.ppermute(value, axis, [(source, source + steps) for source in range(initial, last)])


def broadcast(value, axis, source):
    kept = jnp.where(lax.axis_index(axis) == source, value, 0).astype(value.dtype)
    return lax.psum(kept, axis)


def attend(queries, cand_keys, cand_vals, grad_rows, allowed):
    score_scale = HEAD_SIZE ** (-0.5)
    scores = score_scale * jnp.einsum(
        "tqkgd,tskd->tkgqs", queries, cand_keys, preferred_element_type=jnp.float32
    )
    mask_full = allowed[:, None, None]
    scores = jnp.where(mask_full, scores, -1e30)
    row_max = jnp.max(scores, axis=-1, keepdims=True)
    probs = jnp.where(mask_full, jnp.exp(scores - row_max), 0.0)
    totals = jnp.sum(probs, axis=-1, keepdims=True)
    row_live = jnp.any(allowed, axis=-1)[:, None, None, :, None]
    probs = probs / jnp.where(row_live, totals, 1.0)
    probs_low = probs.astype(jnp.bfloat16)
    attended = jnp.einsum(
        "tkgqs,tskd->tqkgd", probs_low, cand_vals, preferred_element_type=jnp.float32
    )
    row_dot = jnp.sum(grad_rows * attended, axis=-1).transpose(0, 2, 3, 1)[..., None]
    grad_probs = jnp.einsum(
        "tqkgd,tskd->tkgqs", grad_rows, cand_vals, preferred_element_type=jnp.float32
    )
    grad_scores = (probs * (grad_probs - row_dot)).astype(jnp.bfloat16)
    grad_query = score_scale * jnp.einsum(
        "tkgqs,tskd->tqkgd", grad_scores, cand_keys, preferred_element_type=jnp.float32
    )
    grad_key = score_scale * jnp.einsum(
        "tkgqs,tqkgd->tskd", grad_scores, queries, preferred_element_type=jnp.float32
    )
    grad_value = jnp.einsum(
        "tkgqs,tqkgd->tskd", probs_low, grad_rows, preferred_element_type=jnp.float32
    )
    return (grad_query, grad_key, grad_value)


def body(query_in, key_in, value_rows_input, grad_out, query_bias, key_blocks, trace_len):
    ctx_count = lax.axis_size("ctx")
    rank_ctx = lax.axis_index("ctx")
    traces = query_in.shape[0]
    width_kv = key_in.shape[-1]
    width_q = query_in.shape[-1]
    heads_kv = width_kv // HEAD_SIZE
    group_size = width_q // width_kv
    cand_count = PROMPT + WINDOW + 1
    kv_pair = jnp.concatenate([key_in, value_rows_input], axis=-1).reshape(
        traces, 2, BLOCK, 2 * width_kv
    )
    own_ids = jnp.stack([rank_ctx, 2 * ctx_count - 1 - rank_ctx])
    half_count = kv_pair.shape[1]
    from_lower = jnp.stack([from_behind(kv_pair, "ctx", offset) for offset in range(1, WINDOW + 1)])
    from_upper = jnp.stack(
        [from_behind(kv_pair, "ctx", -offset) for offset in range(1, WINDOW + 1)]
    )
    offsets = jnp.arange(1, WINDOW + 1, dtype=jnp.int32)
    lower_dev = rank_ctx - offsets
    upper_dev = rank_ctx + offsets
    lower_ids = jnp.stack([lower_dev, 2 * ctx_count - 1 - lower_dev], axis=1)
    upper_ids = jnp.stack([upper_dev, 2 * ctx_count - 1 - upper_dev], axis=1)
    lower_ids = jnp.where((lower_dev >= 0)[:, None], lower_ids, -1000).reshape(-1)
    upper_ids = jnp.where((upper_dev < ctx_count)[:, None], upper_ids, -1000).reshape(-1)
    lower_data = from_lower.transpose(1, 0, 2, 3, 4).reshape(
        traces, WINDOW * half_count, BLOCK, 2 * width_kv
    )
    upper_data = from_upper.transpose(1, 0, 2, 3, 4).reshape(
        traces, WINDOW * half_count, BLOCK, 2 * width_kv
    )
    data_list = [kv_pair, lower_data, upper_data]
    id_list = [own_ids, lower_ids, upper_ids]
    slot_data = jnp.concatenate(data_list, axis=1)
    slot_ids = jnp.concatenate(id_list)
    targets = own_ids[:, None] - jnp.arange(WINDOW + 1, dtype=jnp.int32)[None]
    chooser = (slot_ids[None, None, :] == targets[..., None]).astype(jnp.bfloat16)
    window_kv = jnp.einsum(
        "jdn,tnbf->tjdbf", chooser, slot_data, preferred_element_type=jnp.float32
    ).astype(jnp.bfloat16)
    first_half = kv_pair[:, 0]
    prompt_kv = jnp.stack(
        [broadcast(first_half, "ctx", source) for source in range(PROMPT)], axis=1
    )
    block_rows = jnp.take(key_blocks, own_ids, axis=1)
    queries = (
        (query_in.astype(jnp.float32) + query_bias)
        .astype(jnp.bfloat16)
        .reshape(traces, 2, BLOCK, heads_kv, group_size, HEAD_SIZE)
    )
    grad_rows = grad_out.reshape(traces, 2, BLOCK, heads_kv, group_size, HEAD_SIZE)
    prompt_grad = jnp.zeros((traces, PROMPT, BLOCK, 2 * width_kv), jnp.float32)
    slot_grad = jnp.zeros((traces, slot_data.shape[1], BLOCK, 2 * width_kv), jnp.float32)
    query_parts = []
    for half_idx in range(2):
        block_here = own_ids[half_idx]
        candidates = jnp.concatenate([prompt_kv, window_kv[:, half_idx]], axis=1)
        cand_keys = candidates[..., :width_kv].reshape(
            traces, cand_count * BLOCK, heads_kv, HEAD_SIZE
        )
        cand_vals = candidates[..., width_kv:].reshape(
            traces, cand_count * BLOCK, heads_kv, HEAD_SIZE
        )
        key_ids = jnp.concatenate(
            [
                jnp.arange(PROMPT, dtype=jnp.int32),
                block_here - jnp.arange(WINDOW + 1, dtype=jnp.int32),
            ]
        )
        prompt_ok = jnp.concatenate(
            [
                jnp.arange(PROMPT, dtype=jnp.int32) < block_here - WINDOW,
                jnp.ones((WINDOW + 1,), jnp.bool_),
            ]
        )
        block_ok = (block_rows[:, half_idx] >= 0) & prompt_ok[None]
        key_pos = (key_ids[:, None] * BLOCK + jnp.arange(BLOCK, dtype=jnp.int32)[None]).reshape(-1)
        query_pos = block_here * BLOCK + jnp.arange(BLOCK, dtype=jnp.int32)
        length = trace_len[:, None, None]
        allowed = (
            jnp.repeat(block_ok, BLOCK, axis=1)[:, None, :]
            & (key_pos[None, None, :] <= query_pos[None, :, None])
            & (key_pos[None, None, :] < length)
            & (query_pos[None, :, None] < length)
        )
        grad_query, grad_key, grad_value = attend(
            queries[:, half_idx], cand_keys, cand_vals, grad_rows[:, half_idx], allowed
        )
        query_parts.append(grad_query)
        contrib = jnp.concatenate(
            [
                grad_key.reshape(traces, cand_count, BLOCK, width_kv),
                grad_value.reshape(traces, cand_count, BLOCK, width_kv),
            ],
            axis=-1,
        )
        prompt_grad = prompt_grad + contrib[:, :PROMPT]
        slot_grad = slot_grad + jnp.einsum(
            "dn,tdbf->tnbf",
            chooser[half_idx].astype(jnp.float32),
            contrib[:, PROMPT:],
            precision=lax.Precision.HIGHEST,
        )
    span = WINDOW * half_count
    own_grad = slot_grad[:, 0:2]
    lower_grad = (
        slot_grad[:, 2 : 2 + span]
        .reshape(traces, WINDOW, half_count, BLOCK, 2 * width_kv)
        .transpose(1, 0, 2, 3, 4)
    )
    upper_grad = (
        slot_grad[:, 2 + span : 2 + 2 * span]
        .reshape(traces, WINDOW, half_count, BLOCK, 2 * width_kv)
        .transpose(1, 0, 2, 3, 4)
    )
    low_part = jnp.zeros_like(lower_grad[0])
    up_part = jnp.zeros_like(upper_grad[0])
    for offset in range(1, WINDOW + 1):
        low_part = low_part + from_behind(lower_grad[offset - 1], "ctx", -offset)
        up_part = up_part + from_behind(upper_grad[offset - 1], "ctx", offset)
    kv_grad = own_grad + low_part + up_part
    owners = jnp.arange(PROMPT, dtype=jnp.int32)
    query_all = jnp.stack(query_parts, axis=1)
    local_bias = jnp.sum(query_all, axis=(0, 1, 2)).reshape(width_q)
    shared_total = lax.psum(prompt_grad, "ctx")
    bias_total = lax.psum(local_bias, ("ctx", "dp"))
    owned = (owners == rank_ctx).astype(jnp.float32)
    kv_grad = kv_grad.at[:, 0].add(jnp.sum(owned[None, :, None, None] * shared_total, axis=1))
    grad_query_out = query_all.reshape(traces, 2 * BLOCK, width_q).astype(jnp.bfloat16)
    grad_key_out = kv_grad[..., :width_kv].reshape(traces, 2 * BLOCK, width_kv).astype(jnp.bfloat16)
    grad_value_out = (
        kv_grad[..., width_kv:].reshape(traces, 2 * BLOCK, width_kv).astype(jnp.bfloat16)
    )
    all_traces = traces * lax.axis_size("dp")
    bias_out = bias_total / math.sqrt(all_traces * 2 * BLOCK * ctx_count)
    return (grad_query_out, grad_key_out, grad_value_out, bias_out)


def solution(mesh):
    return jax.shard_map(
        body,
        mesh=mesh,
        in_specs=(
            P("dp", "ctx", None),
            P("dp", "ctx", None),
            P("dp", "ctx", None),
            P("dp", "ctx", None),
            P(),
            P("dp", None, None),
            P("dp"),
        ),
        out_specs=(P("dp", "ctx", None), P("dp", "ctx", None), P("dp", "ctx", None), P()),
        check_vma=False,
    )
```

profile of v0, /device:TPU:2, one launch (start us, length us, event | category | flops | bytes accessed | tf_op | source)
XLA Modules:
  0.0 588.3 jit_solution(5824512596889643687)
XLA Ops:
  9.7 4.2 collective-permute-start.4
  15.9 4.8 collective-permute-start.2
  35.2 2.9 fusion.73
  38.3 3.7 collective-permute-start
  42.5 3.3 fusion.74
  48.9 4.4 collective-permute-done
  55.6 2.7 convert_bitcast_fusion
  60.0 162.5 %all-reduce.8.cloned.1.call-done = (bf16[1,1,128,1024]{3,1,2,0:T(2,128)(2,1)}, bf16[1,1,128,1024]{3,1,2,0:T(2,128)(2,1)}) async-done(((bf16[1,1,128,1024]{3,1,2,0:T(2,128)(2,1)}, bf16[1,1,128,1024]{3,1,2,0:T(2,128)(2,1)}), (bf16[1,1,128,1024]{3,1,2,0:T(2,128)(2,1)}, bf16[1,1,128,1024]{3,1,2,0:T(2,128)(2,1)})) %all-reduce.8.cloned.1.call-update) | async-done | bytes 524304 | tf_op jit(solution)/shard_map/psum | solution.py:21
  222.5 4.6 pad_maximum_fusion
  233.5 2.7 fusion.75
  248.8 3.2 fusion.9
  252.0 5.3 fusion.40
  257.4 5.2 fusion.29
  262.6 7.1 %fusion.11 = bf16[4,8,128,768]{2,3,1,0:T(8,128)(2,1)S(1)} fusion(f32[4,8,128]{2,1,0:T(8,128)S(1)} %bitcast.338, f32[4,8,128]{2,1,0:T(8,128)S(1)} %broadcast_select_fusion.2, f32[4,8,128]{2,1,0:T(8,128)S(1)} %get-tuple-element.46, f32[4,768,128,8]{2,1,3,0:T(8,128)S(1)} %get-tuple-element.47, pred[128,768]{0,1:T(8,128)(4,1)S(1)} %and_and_fusion, ...), kind=kOutput, calls=%fused_computation.19 | convolution fusion | flops 830472192 | bytes 20856832 | tf_op jit(solution)/shard_map/tqkgd,tskd->tkgqs/dot_general | solution.py:41
  272.8 3.4 fusion.35
  276.2 2.8 copy.106
  279.0 3.7 copy_dynamic-update-slice_fusion.1
  285.1 3.2 fusion.7
  288.4 4.8 fusion.37
  293.2 5.2 fusion.30
  298.4 7.3 %fusion.10 = bf16[4,8,128,768]{2,3,1,0:T(8,128)(2,1)S(1)} fusion(f32[4,8,128]{2,1,0:T(8,128)S(1)} %bitcast.339, f32[4,8,128]{2,1,0:T(8,128)S(1)} %broadcast_select_fusion.3, f32[4,8,128]{2,1,0:T(8,128)S(1)} %get-tuple-element.48, f32[4,768,128,8]{2,1,3,0:T(8,128)S(1)} %get-tuple-element.49, pred[128,768]{0,1:T(8,128)(4,1)S(1)} %and_and_fusion.1, ...), kind=kOutput, calls=%fused_computation.18 | convolution fusion | flops 830472192 | bytes 20856832 | tf_op jit(solution)/shard_map/tqkgd,tskd->tkgqs/dot_general | solution.py:41
  308.8 3.4 fusion.36
  318.2 6.9 %fusion.28 = f32[128,1024,14]{1,2,0:T(8,128)} fusion(f32[1,6,128,1024]{3,1,2,0:T(8,128)S(1)} %copy_dynamic-update-slice_fusion.2, pred[2,4,14]{2,1,0:T(4,128)(4,1)S(1)} %copy-done.26), kind=kOutput, calls=%fused_computation.40 | convolution fusion | flops 88080384 | bytes 9437696 | tf_op jit(solution)/shard_map/dn,tdbf->tnbf/dot_general | solution.py:154
  330.1 10.6 %add_bitcast_fusion = f32[1,14,128,1024]{3,1,2,0:T(8,128)S(1)} fusion(f32[128,1024,14]{1,2,0:T(8,128)} %fusion.28, f32[1,6,128,1024]{3,1,2,0:T(8,128)} %copy-done.4, pred[2,4,14]{2,1,0:T(4,128)(4,1)S(1)} %copy-done.26), kind=kOutput, calls=%fused_computation.17 | convolution fusion | flops 89915392 | bytes 17826304 | tf_op jit(solution)/shard_map/dn,tdbf->tnbf/dot_general | solution.py:154
  340.8 3.6 fusion.71
  350.4 3.0 collective-permute-start.10
  353.4 4.5 collective-permute-start.9
  365.1 23.8 %collective-permute-done.7 = f32[1,2,128,1024]{3,1,2,0:T(2,128)S(1)} collective-permute-done((f32[1,2,128,1024]{3,1,2,0:T(2,128)S(1)}, f32[1,2,128,1024]{3,1,2,0:T(2,128)S(1)}, u32[]{:S(2)}, u32[]{:S(2)}) %collective-permute-start.7) | collective-permute-done | bytes 1048608 | tf_op jit(solution)/shard_map/ppermute | solution.py:16
  395.0 95.3 %psum.31 = f32[4096]{0:T(1024)S(1)} all-reduce(f32[4096]{0:T(1024)S(1)} %add_bitcast_fusion.1), channel_id=1, replica_groups=mesh['ctx'=64,'dp'=4] {'ctx','dp'}, use_global_device_ids=true, to_apply=%region_14.15 | all-reduce | flops 4096 | bytes 32768 | tf_op jit(solution)/shard_map/psum | solution.py:182
  490.9 75.6 %all-reduce.6.cloned.1.call-done = f32[1,2,128,1024]{3,1,2,0:T(2,128)} async-done(((f32[1,2,128,1024]{3,1,2,0:T(2,128)}), f32[1,2,128,1024]{3,1,2,0:T(2,128)}) %all-reduce.6.cloned.1.call-update) | async-done | bytes 1048592 | tf_op jit(solution)/shard_map/psum | solution.py:181
  569.2 5.6 fusion.45
  575.4 3.7 scatter-add.4
  (170 shorter events, 89.5 us)
Async XLA Ops:
  7.2 20.2 %copy-start.13 = (bf16[1,256,4096]{2,1,0:T(8,128)(2,1)S(1)}, bf16[1,256,4096]{2,1,0:T(8,128)(2,1)}, u32[]{:S(2)}) copy-start(bf16[1,256,4096]{2,1,0:T(8,128)(2,1)} %param.9) | copy-start | bytes 6291460
  7.2 215.4 %all-reduce.8.cloned.1.call-start = ((), (), s32[]{:S(2)}) async-start(), calls=%async_computation.1 | async-start | bytes 2097152 | tf_op jit(solution)/shard_map/psum | solution.py:21
  8.4 29.9 %collective-permute-start.5 = (bf16[1,2,128,1024]{3,2,1,0:T(8,128)(2,1)S(1)}, bf16[1,2,128,1024]{3,2,1,0:T(8,128)(2,1)}, u32[]{:S(2)}, u32[]{:S(2)}) collective-permute-start(bf16[1,2,128,1024]{3,2,1,0:T(8,128)(2,1)S(1)} %bitcast.327), channel_id=1, source_target_pairs={{12,0},{16,4},{20,8},{24,12},{28,16},{32,20},{36,24},{40,28},{44,3... | collective-permute-start | bytes 1572872 | tf_op jit(solution)/shard_map/ppermute | solution.py:16
  9.7 36.0 %collective-permute-start.4 = (bf16[1,2,128,1024]{3,2,1,0:T(8,128)(2,1)S(1)}, bf16[1,2,128,1024]{3,2,1,0:T(8,128)(2,1)}, u32[]{:S(2)}, u32[]{:S(2)}) collective-permute-start(bf16[1,2,128,1024]{3,2,1,0:T(8,128)(2,1)S(1)} %bitcast.328), channel_id=1, source_target_pairs={{8,0},{12,4},{16,8},{20,12},{24,16},{28,20},{32,24},{36,28},{40,32... | collective-permute-start | bytes 1572872 | tf_op jit(solution)/shard_map/ppermute | solution.py:16
  13.9 31.8 %collective-permute-start.3 = (bf16[1,2,128,1024]{3,2,1,0:T(8,128)(2,1)S(1)}, bf16[1,2,128,1024]{3,2,1,0:T(8,128)(2,1)}, u32[]{:S(2)}, u32[]{:S(2)}) collective-permute-start(bf16[1,2,128,1024]{3,2,1,0:T(8,128)(2,1)S(1)} %bitcast.329), channel_id=1, source_target_pairs={{4,0},{8,4},{12,8},{16,12},{20,16},{24,20},{28,24},{32,28},{36,32}... | collective-permute-start | bytes 1572872 | tf_op jit(solution)/shard_map/ppermute | solution.py:16
  15.9 32.3 %collective-permute-start.2 = (bf16[1,2,128,1024]{3,2,1,0:T(8,128)(2,1)S(1)}, bf16[1,2,128,1024]{3,2,1,0:T(8,128)(2,1)}, u32[]{:S(2)}, u32[]{:S(2)}) collective-permute-start(bf16[1,2,128,1024]{3,2,1,0:T(8,128)(2,1)S(1)} %bitcast.330), channel_id=1, source_target_pairs={{0,12},{4,16},{8,20},{12,24},{16,28},{20,32},{24,36},{28,40},{32,4... | collective-permute-start | bytes 1572872 | tf_op jit(solution)/shard_map/ppermute | solution.py:16
  20.7 28.1 %collective-permute-start.1 = (bf16[1,2,128,1024]{3,2,1,0:T(8,128)(2,1)S(1)}, bf16[1,2,128,1024]{3,2,1,0:T(8,128)(2,1)}, u32[]{:S(2)}, u32[]{:S(2)}) collective-permute-start(bf16[1,2,128,1024]{3,2,1,0:T(8,128)(2,1)S(1)} %bitcast.331), channel_id=1, source_target_pairs={{0,8},{4,12},{8,16},{12,20},{16,24},{20,28},{24,32},{28,36},{32,40... | collective-permute-start | bytes 1572872 | tf_op jit(solution)/shard_map/ppermute | solution.py:16
  25.0 541.6 %all-reduce.6.cloned.1.call-start = ((), (), s32[]{:S(2)}) async-start(), calls=%async_computation | async-start | bytes 2097152 | tf_op jit(solution)/shard_map/psum | solution.py:181
  32.8 22.8 %copy-start.25 = (pred[2,4,14]{2,1,0:T(4,128)(4,1)}, pred[2,4,14]{2,1,0:T(4,128)(4,1)S(1)}, u32[]{:S(2)}) copy-start(pred[2,4,14]{2,1,0:T(4,128)(4,1)S(1)} %broadcast_compare_fusion.2) | copy-start | bytes 340
  38.1 208.3 %copy-start.9 = (bf16[1,1,128,4,8,128]{5,4,3,2,1,0:T(8,128)(2,1)}, bf16[1,1,128,4,8,128]{5,4,3,2,1,0:T(8,128)(2,1)S(1)}, u32[]{:S(2)}) copy-start(bf16[1,1,128,4,8,128]{5,4,3,2,1,0:T(8,128)(2,1)S(1)} %get-tuple-element.29) | copy-start | bytes 3145732
  38.3 15.0 %collective-permute-start = (bf16[1,2,128,1024]{3,2,1,0:T(8,128)(2,1)S(1)}, bf16[1,2,128,1024]{3,2,1,0:T(8,128)(2,1)S(1)}, u32[]{:S(2)}, u32[]{:S(2)}) collective-permute-start(bf16[1,2,128,1024]{3,2,1,0:T(8,128)(2,1)S(1)} %bitcast.333), channel_id=1, source_target_pairs={{0,4},{4,8},{8,12},{12,16},{16,20},{20,24},{24,28},{28,32},{32,36}... | collective-permute-start | bytes 1572872 | tf_op jit(solution)/shard_map/ppermute | solution.py:16
  239.1 9.7 %copy-start.5 = (bf16[768,4,128]{2,1,0:T(4,128)(2,1)}, bf16[768,4,128]{2,1,0:T(4,128)(2,1)S(1)}, u32[]{:S(2)}) copy-start(bf16[768,4,128]{2,1,0:T(4,128)(2,1)S(1)} %reshape.1055) | copy-start | bytes 2359300
  252.0 5.3 copy-start.24
  262.6 7.1 %copy-start.15 = (f32[1,768,4,128]{3,1,2,0:T(8,128)S(1)}, f32[1,768,4,128]{3,1,2,0:T(8,128)}, u32[]{:S(2)}) copy-start(f32[1,768,4,128]{3,1,2,0:T(8,128)} %fusion.40) | copy-start | bytes 4718596
  262.6 10.2 %copy-start.10 = (bf16[1,1,128,4,8,128]{5,4,3,2,1,0:T(8,128)(2,1)S(1)}, bf16[1,1,128,4,8,128]{5,4,3,2,1,0:T(8,128)(2,1)}, u32[]{:S(2)}) copy-start(bf16[1,1,128,4,8,128]{5,4,3,2,1,0:T(8,128)(2,1)} %copy-done.9) | copy-start | bytes 3145732
  276.2 6.6 %copy-start.7 = (bf16[1,1,128,4,8,128]{5,4,3,2,1,0:T(8,128)(2,1)S(1)}, bf16[1,1,128,4,8,128]{5,4,3,2,1,0:T(8,128)(2,1)}, u32[]{:S(2)}) copy-start(bf16[1,1,128,4,8,128]{5,4,3,2,1,0:T(8,128)(2,1)} %get-tuple-element.28) | copy-start | bytes 3145732
  298.3 7.3 %copy-start.16 = (f32[1,768,4,128]{3,1,2,0:T(8,128)S(1)}, f32[1,768,4,128]{3,1,2,0:T(8,128)}, u32[]{:S(2)}) copy-start(f32[1,768,4,128]{3,1,2,0:T(8,128)} %fusion.37) | copy-start | bytes 4718596
  298.4 10.5 %copy-start.8 = (bf16[1,1,128,4,8,128]{5,4,3,2,1,0:T(8,128)(2,1)S(1)}, bf16[1,1,128,4,8,128]{5,4,3,2,1,0:T(8,128)(2,1)}, u32[]{:S(2)}) copy-start(bf16[1,1,128,4,8,128]{5,4,3,2,1,0:T(8,128)(2,1)} %get-tuple-element.28) | copy-start | bytes 3145732
  312.2 6.0 %copy-start.26 = (pred[2,4,14]{2,1,0:T(4,128)(4,1)S(1)}, pred[2,4,14]{2,1,0:T(4,128)(4,1)}, u32[]{:S(2)}) copy-start(pred[2,4,14]{2,1,0:T(4,128)(4,1)} %copy-done.25) | copy-start | bytes 340
  318.2 6.9 %copy-start.3 = (f32[1,6,128,1024]{3,1,2,0:T(8,128)S(1)}, f32[1,6,128,1024]{3,1,2,0:T(8,128)}, u32[]{:S(2)}) copy-start(f32[1,6,128,1024]{3,1,2,0:T(8,128)} %copy_dynamic-update-slice_fusion.1) | copy-start | bytes 9437188
  318.2 6.9 %copy-start.11 = (f32[1,768,4,128]{3,2,0,1:T(4,128)S(1)}, f32[1,768,4,128]{3,2,0,1:T(4,128)}, u32[]{:S(2)}) copy-start(f32[1,768,4,128]{3,2,0,1:T(4,128)} %copy.107) | copy-start | bytes 4718596
  328.1 31.9 %slice-start = ((s8[6291456]{0:T(1024)(128)(4,1)}), s8[2097152]{0:T(1024)(128)(4,1)S(1)}, s32[]{:S(2)}) async-start(s8[6291456]{0:T(1024)(128)(4,1)} %bitcast.308), calls=%async_computation.2 | async-start | bytes 4194304
  330.1 29.8 %slice-start.1 = ((s8[6291456]{0:T(1024)(128)(4,1)}), s8[4194304]{0:T(1024)(128)(4,1)S(1)}, s32[]{:S(2)}) async-start(s8[6291456]{0:T(1024)(128)(4,1)} %bitcast.308), calls=%async_computation.3 | async-start | bytes 8388608
  340.8 19.2 %copy-start.6 = (bf16[768,4,128]{2,1,0:T(4,128)(2,1)S(1)}, bf16[768,4,128]{2,1,0:T(4,128)(2,1)}, u32[]{:S(2)}) copy-start(bf16[768,4,128]{2,1,0:T(4,128)(2,1)} %copy-done.5) | copy-start | bytes 2359300
  345.6 43.2 %collective-permute-start.7 = (f32[1,2,128,1024]{3,1,2,0:T(2,128)S(1)}, f32[1,2,128,1024]{3,1,2,0:T(2,128)S(1)}, u32[]{:S(2)}, u32[]{:S(2)}) collective-permute-start(f32[1,2,128,1024]{3,1,2,0:T(2,128)S(1)} %get-tuple-element.20), channel_id=1, source_target_pairs={{8,0},{12,4},{16,8},{20,12},{24,16},{28,20},{32,24},{36,28},{40,32... | collective-permute-start | bytes 3145736 | tf_op jit(solution)/shard_map/ppermute | solution.py:16
  348.1 221.1 %collective-permute-start.11 = (f32[1,2,128,1024]{3,1,2,0:T(2,128)}, f32[1,2,128,1024]{3,1,2,0:T(2,128)}, u32[]{:S(2)}, u32[]{:S(2)}) collective-permute-start(f32[1,2,128,1024]{3,1,2,0:T(2,128)} %get-tuple-element.21), channel_id=1, source_target_pairs={{0,12},{4,16},{8,20},{12,24},{16,28},{20,32},{24,36},{28,40},{32,4... | collective-permute-start | bytes 3145736 | tf_op jit(solution)/shard_map/ppermute | solution.py:16
  350.4 218.7 %collective-permute-start.10 = (f32[1,2,128,1024]{3,1,2,0:T(2,128)}, f32[1,2,128,1024]{3,1,2,0:T(2,128)}, u32[]{:S(2)}, u32[]{:S(2)}) collective-permute-start(f32[1,2,128,1024]{3,1,2,0:T(2,128)} %get-tuple-element.22), channel_id=1, source_target_pairs={{0,8},{4,12},{8,16},{12,20},{16,24},{20,28},{24,32},{28,36},{32,40... | collective-permute-start | bytes 3145736 | tf_op jit(solution)/shard_map/ppermute | solution.py:16
  353.4 215.8 %collective-permute-start.9 = (f32[1,2,128,1024]{3,1,2,0:T(2,128)}, f32[1,2,128,1024]{3,1,2,0:T(2,128)}, u32[]{:S(2)}, u32[]{:S(2)}) collective-permute-start(f32[1,2,128,1024]{3,1,2,0:T(2,128)} %get-tuple-element.23), channel_id=1, source_target_pairs={{0,4},{4,8},{8,12},{12,16},{16,20},{20,24},{24,28},{28,32},{32,36}... | collective-permute-start | bytes 3145736 | tf_op jit(solution)/shard_map/ppermute | solution.py:16
  357.9 211.2 %collective-permute-start.8 = (f32[1,2,128,1024]{3,1,2,0:T(2,128)}, f32[1,2,128,1024]{3,1,2,0:T(2,128)}, u32[]{:S(2)}, u32[]{:S(2)}) collective-permute-start(f32[1,2,128,1024]{3,1,2,0:T(2,128)} %get-tuple-element.24), channel_id=1, source_target_pairs={{12,0},{16,4},{20,8},{24,12},{28,16},{32,20},{36,24},{40,28},{44,3... | collective-permute-start | bytes 3145736 | tf_op jit(solution)/shard_map/ppermute | solution.py:16
  388.9 180.3 %collective-permute-start.6 = (f32[1,2,128,1024]{3,1,2,0:T(2,128)}, f32[1,2,128,1024]{3,1,2,0:T(2,128)}, u32[]{:S(2)}, u32[]{:S(2)}) collective-permute-start(f32[1,2,128,1024]{3,1,2,0:T(2,128)} %get-tuple-element.25), channel_id=1, source_target_pairs={{4,0},{8,4},{12,8},{16,12},{20,16},{24,20},{28,24},{32,28},{36,32}... | collective-permute-start | bytes 3145736 | tf_op jit(solution)/shard_map/ppermute | solution.py:16
  391.1 175.4 %copy-start.27 = (f32[2]{0:T(128)S(1)}, f32[2]{0:T(128)}, u32[]{:S(2)}) copy-start(f32[2]{0:T(128)} %compare_convert_fusion) | copy-start | bytes 28
  392.7 176.5 %copy-start.22 = (f32[1,2,128,1024]{3,1,2,0:T(2,128)S(1)}, f32[1,2,128,1024]{3,1,2,0:T(2,128)}, u32[]{:S(2)}) copy-start(f32[1,2,128,1024]{3,1,2,0:T(2,128)} %copy-done.21) | copy-start | bytes 3145732
  (14 other events, 55.1 us)
Sparse Core Ops, SparseCore 0:
  25.1 197.4 all-reduce.7
  330.3 236.2 all-reduce.5
where the time goes:
time: 595 us; the launch traced here: 588 us
  waiting for transfers between devices  267 us (45%)
  blocking collectives  95.3 us (16%)
  matrix products  71.3 us (12%)
  local copies, waits for them, and re-layouts  70.5 us (12%)
  other arithmetic  34.4 us (6%)
  starting transfers between devices  34.1 us (6%)
  between operations  15.7 us (3%)
    psum x1, waiting for transfers between devices, broadcast(): return lax.psum(kept, axis)  163 us
    psum x1, blocking collectives, body(): bias_total = lax.psum(local_bias, ('ctx', 'dp'))  95.3 us
    psum x1, waiting for transfers between devices, body(): shared_total = lax.psum(prompt_grad, 'ctx')  75.6 us
    ppermute x12, starting transfers between devices, from_behind(): lax.ppermute(value, axis, [(source, source + steps) for source in range(i...  34 us
    ppermute x12, waiting for transfers between devices, from_behind(): lax.ppermute(value, axis, [(source, source + steps) for source in range(i...  28.9 us
    dot_general x2, matrix products, body(): jnp.einsum('dn,tdbf->tnbf', chooser[half_idx].astype(jnp.float32), contri...  17.5 us
    unnamed x69, local copies, waits for them, and re-layouts  14.9 us
    dot_general x2, matrix products, attend(): jnp.einsum('tqkgd,tskd->tkgqs', grad_rows, cand_vals, preferred_element_t...  14.4 us
  transfers between devices with their start and end apart: 14, of which 5 were waited for; matrix products, arithmetic and copies ran while one was open for 9% of the time, Pallas kernels for 0%

commit v1 on v0

--- a/solution.py
+++ b/solution.py
@@ -179,7 +179,9 @@
     query_all = jnp.stack(query_parts, axis=1)
     local_bias = jnp.sum(query_all, axis=(0, 1, 2)).reshape(width_q)
     shared_total = lax.psum(prompt_grad, "ctx")
-    bias_total = lax.psum(local_bias, ("ctx", "dp"))
+    bias_total = local_bias
+    for mesh_axis in ("dp", "ctx"):
+        bias_total = lax.psum(bias_total, mesh_axis)
     owned = (owners == rank_ctx).astype(jnp.float32)
     kv_grad = kv_grad.at[:, 0].add(jnp.sum(owned[None, :, None, None] * shared_total, axis=1))
     grad_query_out = query_all.reshape(traces, 2 * BLOCK, width_q).astype(jnp.bfloat16)

time: 595 us -> 687 us (1.15)
  blocking collectives: 95.3 us -> 260 us
  waiting for transfers between devices: 267 us -> 191 us
    psum x1 -> x2, blocking collectives: 95.3 us -> 260 us  [body(): bias_total = lax.psum(bias_total, mesh_axis)]
    psum x1, waiting for transfers between devices: 75.6 us -> 0.01 us  [body(): shared_total = lax.psum(prompt_grad, 'ctx')]
  transfers between devices with their start and end apart: 14 -> 14, of which waited for: 5 -> 4; matrix products, arithmetic and copies ran while one was open for 9% -> 8% of each run, Pallas kernels for 0% -> 0%
where the time goes in v1:
time: 687 us; the launch traced here: 677 us
  blocking collectives  260 us (38%)
  waiting for transfers between devices  191 us (28%)
  matrix products  71.3 us (10%)
  local copies, waits for them, and re-layouts  70.6 us (10%)
  other arithmetic  34.3 us (5%)
  starting transfers between devices  34.1 us (5%)
  between operations  15.7 us (2%)
    psum x2, blocking collectives, body(): bias_total = lax.psum(bias_total, mesh_axis)  260 us
    psum x1, waiting for transfers between devices, broadcast(): return lax.psum(kept, axis)  163 us
    ppermute x12, starting transfers between devices, from_behind(): lax.ppermute(value, axis, [(source, source + steps) for source in range(i...  34 us
    ppermute x12, waiting for transfers between devices, from_behind(): lax.ppermute(value, axis, [(source, source + steps) for source in range(i...  28.9 us
    dot_general x2, matrix products, body(): jnp.einsum('dn,tdbf->tnbf', chooser[half_idx].astype(jnp.float32), contri...  17.5 us
    unnamed x69, local copies, waits for them, and re-layouts  14.9 us
    dot_general x2, matrix products, attend(): jnp.einsum('tqkgd,tskd->tkgqs', grad_rows, cand_vals, preferred_element_t...  14.4 us
  transfers between devices with their start and end apart: 14, of which 4 were waited for; matrix products, arithmetic and copies ran while one was open for 8% of the time, Pallas kernels for 0%

profile of v1, /device:TPU:2, one launch (start us, length us, event | category | flops | bytes accessed | tf_op | source)
XLA Modules:
  0.0 677.1 jit_solution(3771687152625029068)
XLA Ops:
  9.7 4.2 collective-permute-start.4
  15.9 4.8 collective-permute-start.2
  35.2 2.9 fusion.73
  38.3 3.7 collective-permute-start
  42.5 3.3 fusion.74
  48.8 4.5 collective-permute-done
  55.6 2.7 convert_bitcast_fusion
  60.0 162.5 %all-reduce.8.cloned.1.call-done = (bf16[1,1,128,1024]{3,1,2,0:T(2,128)(2,1)}, bf16[1,1,128,1024]{3,1,2,0:T(2,128)(2,1)}) async-done(((bf16[1,1,128,1024]{3,1,2,0:T(2,128)(2,1)}, bf16[1,1,128,1024]{3,1,2,0:T(2,128)(2,1)}), (bf16[1,1,128,1024]{3,1,2,0:T(2,128)(2,1)}, bf16[1,1,128,1024]{3,1,2,0:T(2,128)(2,1)})) %all-reduce.8.cloned.1.call-update) | async-done | bytes 524304 | tf_op jit(solution)/shard_map/psum | solution.py:21
  222.6 4.6 pad_maximum_fusion
  233.6 2.7 fusion.75
  248.8 3.2 fusion.9
  252.1 5.3 fusion.40
  257.4 5.2 fusion.29
  262.6 7.1 %fusion.11 = bf16[4,8,128,768]{2,3,1,0:T(8,128)(2,1)S(1)} fusion(f32[4,8,128]{2,1,0:T(8,128)S(1)} %bitcast.338, f32[4,8,128]{2,1,0:T(8,128)S(1)} %broadcast_select_fusion.2, f32[4,8,128]{2,1,0:T(8,128)S(1)} %get-tuple-element.46, f32[4,768,128,8]{2,1,3,0:T(8,128)S(1)} %get-tuple-element.47, pred[128,768]{0,1:T(8,128)(4,1)S(1)} %and_and_fusion, ...), kind=kOutput, calls=%fused_computation.19 | convolution fusion | flops 830472192 | bytes 20856832 | tf_op jit(solution)/shard_map/tqkgd,tskd->tkgqs/dot_general | solution.py:41
  272.8 3.4 fusion.35
  276.2 2.8 copy.106
  279.1 3.8 copy_dynamic-update-slice_fusion.1
  285.2 3.2 fusion.7
  288.5 4.8 fusion.37
  293.3 5.2 fusion.30
  298.5 7.3 %fusion.10 = bf16[4,8,128,768]{2,3,1,0:T(8,128)(2,1)S(1)} fusion(f32[4,8,128]{2,1,0:T(8,128)S(1)} %bitcast.339, f32[4,8,128]{2,1,0:T(8,128)S(1)} %broadcast_select_fusion.3, f32[4,8,128]{2,1,0:T(8,128)S(1)} %get-tuple-element.48, f32[4,768,128,8]{2,1,3,0:T(8,128)S(1)} %get-tuple-element.49, pred[128,768]{0,1:T(8,128)(4,1)S(1)} %and_and_fusion.1, ...), kind=kOutput, calls=%fused_computation.18 | convolution fusion | flops 830472192 | bytes 20856832 | tf_op jit(solution)/shard_map/tqkgd,tskd->tkgqs/dot_general | solution.py:41
  308.9 3.4 fusion.36
  318.4 6.9 %fusion.28 = f32[128,1024,14]{1,2,0:T(8,128)} fusion(f32[1,6,128,1024]{3,1,2,0:T(8,128)S(1)} %copy_dynamic-update-slice_fusion.2, pred[2,4,14]{2,1,0:T(4,128)(4,1)S(1)} %copy-done.26), kind=kOutput, calls=%fused_computation.40 | convolution fusion | flops 88080384 | bytes 9437696 | tf_op jit(solution)/shard_map/dn,tdbf->tnbf/dot_general | solution.py:154
  330.3 10.6 %add_bitcast_fusion = f32[1,14,128,1024]{3,1,2,0:T(8,128)S(1)} fusion(f32[128,1024,14]{1,2,0:T(8,128)} %fusion.28, f32[1,6,128,1024]{3,1,2,0:T(8,128)} %copy-done.4, pred[2,4,14]{2,1,0:T(4,128)(4,1)S(1)} %copy-done.26), kind=kOutput, calls=%fused_computation.17 | convolution fusion | flops 89915392 | bytes 17826304 | tf_op jit(solution)/shard_map/dn,tdbf->tnbf/dot_general | solution.py:154
  341.0 3.6 fusion.71
  350.6 3.0 collective-permute-start.10
  353.6 4.5 collective-permute-start.9
  365.3 23.8 %collective-permute-done.7 = f32[1,2,128,1024]{3,1,2,0:T(2,128)S(1)} collective-permute-done((f32[1,2,128,1024]{3,1,2,0:T(2,128)S(1)}, f32[1,2,128,1024]{3,1,2,0:T(2,128)S(1)}, u32[]{:S(2)}, u32[]{:S(2)}) %collective-permute-start.7) | collective-permute-done | bytes 1048608 | tf_op jit(solution)/shard_map/ppermute | solution.py:16
  395.2 16.9 %psum.38 = f32[4096]{0:T(1024)S(1)} all-reduce(f32[4096]{0:T(1024)S(1)} %add_bitcast_fusion.1), channel_id=1, replica_groups=mesh['ctx'=64,'dp'=4] {'dp'}, use_global_device_ids=true, to_apply=%region_14.15 | all-reduce | flops 4096 | bytes 32768 | tf_op jit(solution)/shard_map/psum | solution.py:184
  412.0 242.7 %psum.39 = f32[4096]{0:T(1024)S(1)} all-reduce(f32[4096]{0:T(1024)S(1)} %psum.38), channel_id=1, replica_groups=mesh['ctx'=64,'dp'=4] {'ctx'}, use_global_device_ids=true, to_apply=%region_15.16 | all-reduce | flops 4096 | bytes 32768 | tf_op jit(solution)/shard_map/psum | solution.py:184
  658.0 5.5 fusion.45
  664.1 3.7 scatter-add.4
  (171 shorter events, 89.6 us)
Async XLA Ops:
  7.2 20.2 %copy-start.13 = (bf16[1,256,4096]{2,1,0:T(8,128)(2,1)S(1)}, bf16[1,256,4096]{2,1,0:T(8,128)(2,1)}, u32[]{:S(2)}) copy-start(bf16[1,256,4096]{2,1,0:T(8,128)(2,1)} %param.9) | copy-start | bytes 6291460
  7.2 215.4 %all-reduce.8.cloned.1.call-start = ((), (), s32[]{:S(2)}) async-start(), calls=%async_computation.1 | async-start | bytes 2097152 | tf_op jit(solution)/shard_map/psum | solution.py:21
  8.4 29.9 %collective-permute-start.5 = (bf16[1,2,128,1024]{3,2,1,0:T(8,128)(2,1)S(1)}, bf16[1,2,128,1024]{3,2,1,0:T(8,128)(2,1)}, u32[]{:S(2)}, u32[]{:S(2)}) collective-permute-start(bf16[1,2,128,1024]{3,2,1,0:T(8,128)(2,1)S(1)} %bitcast.327), channel_id=1, source_target_pairs={{12,0},{16,4},{20,8},{24,12},{28,16},{32,20},{36,24},{40,28},{44,3... | collective-permute-start | bytes 1572872 | tf_op jit(solution)/shard_map/ppermute | solution.py:16
  9.7 36.0 %collective-permute-start.4 = (bf16[1,2,128,1024]{3,2,1,0:T(8,128)(2,1)S(1)}, bf16[1,2,128,1024]{3,2,1,0:T(8,128)(2,1)}, u32[]{:S(2)}, u32[]{:S(2)}) collective-permute-start(bf16[1,2,128,1024]{3,2,1,0:T(8,128)(2,1)S(1)} %bitcast.328), channel_id=1, source_target_pairs={{8,0},{12,4},{16,8},{20,12},{24,16},{28,20},{32,24},{36,28},{40,32... | collective-permute-start | bytes 1572872 | tf_op jit(solution)/shard_map/ppermute | solution.py:16
  13.9 31.8 %collective-permute-start.3 = (bf16[1,2,128,1024]{3,2,1,0:T(8,128)(2,1)S(1)}, bf16[1,2,128,1024]{3,2,1,0:T(8,128)(2,1)}, u32[]{:S(2)}, u32[]{:S(2)}) collective-permute-start(bf16[1,2,128,1024]{3,2,1,0:T(8,128)(2,1)S(1)} %bitcast.329), channel_id=1, source_target_pairs={{4,0},{8,4},{12,8},{16,12},{20,16},{24,20},{28,24},{32,28},{36,32}... | collective-permute-start | bytes 1572872 | tf_op jit(solution)/shard_map/ppermute | solution.py:16
  15.9 32.3 %collective-permute-start.2 = (bf16[1,2,128,1024]{3,2,1,0:T(8,128)(2,1)S(1)}, bf16[1,2,128,1024]{3,2,1,0:T(8,128)(2,1)}, u32[]{:S(2)}, u32[]{:S(2)}) collective-permute-start(bf16[1,2,128,1024]{3,2,1,0:T(8,128)(2,1)S(1)} %bitcast.330), channel_id=1, source_target_pairs={{0,12},{4,16},{8,20},{12,24},{16,28},{20,32},{24,36},{28,40},{32,4... | collective-permute-start | bytes 1572872 | tf_op jit(solution)/shard_map/ppermute | solution.py:16
  20.7 28.1 %collective-permute-start.1 = (bf16[1,2,128,1024]{3,2,1,0:T(8,128)(2,1)S(1)}, bf16[1,2,128,1024]{3,2,1,0:T(8,128)(2,1)}, u32[]{:S(2)}, u32[]{:S(2)}) collective-permute-start(bf16[1,2,128,1024]{3,2,1,0:T(8,128)(2,1)S(1)} %bitcast.331), channel_id=1, source_target_pairs={{0,8},{4,12},{8,16},{12,20},{16,24},{20,28},{24,32},{28,36},{32,40... | collective-permute-start | bytes 1572872 | tf_op jit(solution)/shard_map/ppermute | solution.py:16
  25.0 630.4 %all-reduce.6.cloned.1.call-start = ((), (), s32[]{:S(2)}) async-start(), calls=%async_computation | async-start | bytes 2097152 | tf_op jit(solution)/shard_map/psum | solution.py:181
  32.8 22.8 %copy-start.25 = (pred[2,4,14]{2,1,0:T(4,128)(4,1)}, pred[2,4,14]{2,1,0:T(4,128)(4,1)S(1)}, u32[]{:S(2)}) copy-start(pred[2,4,14]{2,1,0:T(4,128)(4,1)S(1)} %broadcast_compare_fusion.2) | copy-start | bytes 340
  38.1 208.3 %copy-start.9 = (bf16[1,1,128,4,8,128]{5,4,3,2,1,0:T(8,128)(2,1)}, bf16[1,1,128,4,8,128]{5,4,3,2,1,0:T(8,128)(2,1)S(1)}, u32[]{:S(2)}) copy-start(bf16[1,1,128,4,8,128]{5,4,3,2,1,0:T(8,128)(2,1)S(1)} %get-tuple-element.29) | copy-start | bytes 3145732
  38.3 15.0 %collective-permute-start = (bf16[1,2,128,1024]{3,2,1,0:T(8,128)(2,1)S(1)}, bf16[1,2,128,1024]{3,2,1,0:T(8,128)(2,1)S(1)}, u32[]{:S(2)}, u32[]{:S(2)}) collective-permute-start(bf16[1,2,128,1024]{3,2,1,0:T(8,128)(2,1)S(1)} %bitcast.333), channel_id=1, source_target_pairs={{0,4},{4,8},{8,12},{12,16},{16,20},{20,24},{24,28},{28,32},{32,36}... | collective-permute-start | bytes 1572872 | tf_op jit(solution)/shard_map/ppermute | solution.py:16
  239.1 9.7 %copy-start.5 = (bf16[768,4,128]{2,1,0:T(4,128)(2,1)}, bf16[768,4,128]{2,1,0:T(4,128)(2,1)S(1)}, u32[]{:S(2)}) copy-start(bf16[768,4,128]{2,1,0:T(4,128)(2,1)S(1)} %reshape.1055) | copy-start | bytes 2359300
  252.1 5.3 copy-start.24
  262.6 7.1 %copy-start.15 = (f32[1,768,4,128]{3,1,2,0:T(8,128)S(1)}, f32[1,768,4,128]{3,1,2,0:T(8,128)}, u32[]{:S(2)}) copy-start(f32[1,768,4,128]{3,1,2,0:T(8,128)} %fusion.40) | copy-start | bytes 4718596
  262.6 10.2 %copy-start.10 = (bf16[1,1,128,4,8,128]{5,4,3,2,1,0:T(8,128)(2,1)S(1)}, bf16[1,1,128,4,8,128]{5,4,3,2,1,0:T(8,128)(2,1)}, u32[]{:S(2)}) copy-start(bf16[1,1,128,4,8,128]{5,4,3,2,1,0:T(8,128)(2,1)} %copy-done.9) | copy-start | bytes 3145732
  276.2 6.6 copy-start.7
  298.5 7.3 %copy-start.16 = (f32[1,768,4,128]{3,1,2,0:T(8,128)S(1)}, f32[1,768,4,128]{3,1,2,0:T(8,128)}, u32[]{:S(2)}) copy-start(f32[1,768,4,128]{3,1,2,0:T(8,128)} %fusion.37) | copy-start | bytes 4718596
  298.5 10.5 %copy-start.8 = (bf16[1,1,128,4,8,128]{5,4,3,2,1,0:T(8,128)(2,1)S(1)}, bf16[1,1,128,4,8,128]{5,4,3,2,1,0:T(8,128)(2,1)}, u32[]{:S(2)}) copy-start(bf16[1,1,128,4,8,128]{5,4,3,2,1,0:T(8,128)(2,1)} %get-tuple-element.28) | copy-start | bytes 3145732
  312.3 6.0 copy-start.26
  318.3 6.9 %copy-start.3 = (f32[1,6,128,1024]{3,1,2,0:T(8,128)S(1)}, f32[1,6,128,1024]{3,1,2,0:T(8,128)}, u32[]{:S(2)}) copy-start(f32[1,6,128,1024]{3,1,2,0:T(8,128)} %copy_dynamic-update-slice_fusion.1) | copy-start | bytes 9437188
  318.4 6.9 %copy-start.11 = (f32[1,768,4,128]{3,2,0,1:T(4,128)S(1)}, f32[1,768,4,128]{3,2,0,1:T(4,128)}, u32[]{:S(2)}) copy-start(f32[1,768,4,128]{3,2,0,1:T(4,128)} %copy.107) | copy-start | bytes 4718596
  328.3 31.9 %slice-start = ((s8[6291456]{0:T(1024)(128)(4,1)}), s8[2097152]{0:T(1024)(128)(4,1)S(1)}, s32[]{:S(2)}) async-start(s8[6291456]{0:T(1024)(128)(4,1)} %bitcast.308), calls=%async_computation.2 | async-start | bytes 4194304
  330.3 29.8 %slice-start.1 = ((s8[6291456]{0:T(1024)(128)(4,1)}), s8[4194304]{0:T(1024)(128)(4,1)S(1)}, s32[]{:S(2)}) async-start(s8[6291456]{0:T(1024)(128)(4,1)} %bitcast.308), calls=%async_computation.3 | async-start | bytes 8388608
  341.0 19.2 %copy-start.6 = (bf16[768,4,128]{2,1,0:T(4,128)(2,1)S(1)}, bf16[768,4,128]{2,1,0:T(4,128)(2,1)}, u32[]{:S(2)}) copy-start(bf16[768,4,128]{2,1,0:T(4,128)(2,1)} %copy-done.5) | copy-start | bytes 2359300
  345.8 43.2 %collective-permute-start.7 = (f32[1,2,128,1024]{3,1,2,0:T(2,128)S(1)}, f32[1,2,128,1024]{3,1,2,0:T(2,128)S(1)}, u32[]{:S(2)}, u32[]{:S(2)}) collective-permute-start(f32[1,2,128,1024]{3,1,2,0:T(2,128)S(1)} %get-tuple-element.20), channel_id=1, source_target_pairs={{8,0},{12,4},{16,8},{20,12},{24,16},{28,20},{32,24},{36,28},{40,32... | collective-permute-start | bytes 3145736 | tf_op jit(solution)/shard_map/ppermute | solution.py:16
  348.3 309.7 %collective-permute-start.11 = (f32[1,2,128,1024]{3,1,2,0:T(2,128)}, f32[1,2,128,1024]{3,1,2,0:T(2,128)}, u32[]{:S(2)}, u32[]{:S(2)}) collective-permute-start(f32[1,2,128,1024]{3,1,2,0:T(2,128)} %get-tuple-element.21), channel_id=1, source_target_pairs={{0,12},{4,16},{8,20},{12,24},{16,28},{20,32},{24,36},{28,40},{32,4... | collective-permute-start | bytes 3145736 | tf_op jit(solution)/shard_map/ppermute | solution.py:16
  350.6 307.4 %collective-permute-start.10 = (f32[1,2,128,1024]{3,1,2,0:T(2,128)}, f32[1,2,128,1024]{3,1,2,0:T(2,128)}, u32[]{:S(2)}, u32[]{:S(2)}) collective-permute-start(f32[1,2,128,1024]{3,1,2,0:T(2,128)} %get-tuple-element.22), channel_id=1, source_target_pairs={{0,8},{4,12},{8,16},{12,20},{16,24},{20,28},{24,32},{28,36},{32,40... | collective-permute-start | bytes 3145736 | tf_op jit(solution)/shard_map/ppermute | solution.py:16
  353.6 304.4 %collective-permute-start.9 = (f32[1,2,128,1024]{3,1,2,0:T(2,128)}, f32[1,2,128,1024]{3,1,2,0:T(2,128)}, u32[]{:S(2)}, u32[]{:S(2)}) collective-permute-start(f32[1,2,128,1024]{3,1,2,0:T(2,128)} %get-tuple-element.23), channel_id=1, source_target_pairs={{0,4},{4,8},{8,12},{12,16},{16,20},{20,24},{24,28},{28,32},{32,36}... | collective-permute-start | bytes 3145736 | tf_op jit(solution)/shard_map/ppermute | solution.py:16
  358.1 299.9 %collective-permute-start.8 = (f32[1,2,128,1024]{3,1,2,0:T(2,128)}, f32[1,2,128,1024]{3,1,2,0:T(2,128)}, u32[]{:S(2)}, u32[]{:S(2)}) collective-permute-start(f32[1,2,128,1024]{3,1,2,0:T(2,128)} %get-tuple-element.24), channel_id=1, source_target_pairs={{12,0},{16,4},{20,8},{24,12},{28,16},{32,20},{36,24},{40,28},{44,3... | collective-permute-start | bytes 3145736 | tf_op jit(solution)/shard_map/ppermute | solution.py:16
  389.0 269.0 %collective-permute-start.6 = (f32[1,2,128,1024]{3,1,2,0:T(2,128)}, f32[1,2,128,1024]{3,1,2,0:T(2,128)}, u32[]{:S(2)}, u32[]{:S(2)}) collective-permute-start(f32[1,2,128,1024]{3,1,2,0:T(2,128)} %get-tuple-element.25), channel_id=1, source_target_pairs={{4,0},{8,4},{12,8},{16,12},{20,16},{24,20},{28,24},{32,28},{36,32}... | collective-permute-start | bytes 3145736 | tf_op jit(solution)/shard_map/ppermute | solution.py:16
  391.3 264.1 %copy-start.27 = (f32[2]{0:T(128)S(1)}, f32[2]{0:T(128)}, u32[]{:S(2)}) copy-start(f32[2]{0:T(128)} %compare_convert_fusion) | copy-start | bytes 28
  392.8 265.2 %copy-start.22 = (f32[1,2,128,1024]{3,1,2,0:T(2,128)S(1)}, f32[1,2,128,1024]{3,1,2,0:T(2,128)}, u32[]{:S(2)}) copy-start(f32[1,2,128,1024]{3,1,2,0:T(2,128)} %copy-done.21) | copy-start | bytes 3145732
  (14 other events, 55.1 us)
Sparse Core Ops, SparseCore 0:
  25.1 197.4 all-reduce.7
  330.4 237.1 all-reduce.5
